TPU v7x, 32 devices: a whole 2x2x4 slice. The times are simulated.
32 devices in a mesh: grp: 2 (over x), row: 16 (over z, y, core).
Axes of the slice: x: 2, y: 2, z: 4, core: 2. Of those that a mesh axis runs over, the one named last changes fastest.
Arguments:
- start_vectors: bfloat16 [64, 73728], P(None, ('grp', 'row')), parts along dimension 1, may hold values from -6 to 6
- blocks: bfloat16 [384, 12, 192, 192], P(('grp', 'row')), parts along dimension 0
- block_cols: int32 [384, 12], P(('grp', 'row')), parts along dimension 0, may hold values from 0 to 191, as said below
- positions: bfloat16 [73728], P(('grp', 'row')), parts along dimension 0, may hold values from -1 to 1
Outputs:
- chebyshev_two: bfloat16 [64, 73728], P(None, ('grp', 'row')), parts along dimension 1
- heat_current: float32 [64, 73728], P(None, ('grp', 'row')), parts along dimension 1
There are 2 independent parts, one for each index of `grp`. A program takes and returns all parts, laid end to end along the dimension named above; each array names one. Nothing has to cross between parts.
Inputs may be any that keep to these rules, and one draw needn't show every extreme that they name: block_cols[c, 0] = c; the other entries of row c are distinct clusters (c + d) mod 192 with d from 1 to 12; some row holds distance 12.
All inputs are finite; a program needn't handle non-finite values.
Results may differ from a plain program's by a relative error of at most 0.012.
Values may be sent and summed in bfloat16 or wider, within the bound.
A program may use at most 128 MiB of HBM per device.

v0:
```python
import jax
import jax.numpy as jnp
from jax import lax
from jax.experimental import pallas as pl
from jax.experimental.pallas import tpu as pltpu
from jax.sharding import PartitionSpec as P

F32 = jnp.float32
BF16 = jnp.bfloat16
STEP = 4


def kernel(cols_ref, v_ref, p_ref, blocks_ref, x2_ref, heat_ref,
           blk, blkt, ze, zo, ee0, eo0, ee1, eo1, ee2, eo2, own, sout, sin,
           pos, pup, tabv, table,
           blk_sem, vs_sem, vr_sem, ss_sem, sr_sem, ps_sem, pr_sem, tab_sem):
    C, K = blocks_ref.shape[0], blocks_ref.shape[1]
    B = blocks_ref.shape[2]
    NV = v_ref.shape[0]
    Q = C // 2
    W = 2 * B
    n = lax.axis_size("row")
    me = lax.axis_index("row")
    nxt, prv = lax.rem(me + 1, n), lax.rem(me + n - 1, n)

    barrier = pltpu.get_barrier_semaphore()
    for neighbour in (prv, nxt):
        pl.semaphore_signal(barrier, inc=1, device_id={"row": neighbour},
                            device_id_type=pl.DeviceIdType.MESH)

    def block_copy(i):
        return pltpu.make_async_copy(
            blocks_ref.at[i], blk.at[i, pl.ds(0, K)], blk_sem.at[i])

    for i in range(C):
        block_copy(i).start()

    clusters = C * n
    off = cols_ref[...] - (me * C + lax.broadcasted_iota(jnp.int32, (C, K), 0))
    off = jnp.where(off < 0, off + clusters, off)
    lane = lax.broadcasted_iota(jnp.int32, (C, 128), 1)
    found = jnp.full((C, 128), K, jnp.int32)
    for k in range(K):
        found = jnp.where(off[:, k:k + 1] == lane, k, found)
    tabv[...] = found
    table_copy = pltpu.make_async_copy(tabv, table, tab_sem)
    table_copy.start()

    for q in range(Q):
        pair = v_ref[:, q * W:(q + 1) * W]
        ee0[q] = pair
        ze[Q + q, :NV] = pair
    pos[...] = jnp.zeros(pos.shape, F32)
    for q in range(Q):
        pos[q:q + 1, :] = p_ref[:, q * W:(q + 1) * W].astype(F32)

    def vec_copy(app, q):
        e = (ee0, ee1, ee2)[app]
        return pltpu.make_async_remote_copy(
            src_ref=e.at[q, pl.ds(0, NV)], dst_ref=e.at[Q + q, pl.ds(0, NV)],
            send_sem=vs_sem.at[app, q], recv_sem=vr_sem.at[app, q],
            device_id={"row": prv}, device_id_type=pl.DeviceIdType.MESH)

    def spill_copy(app, q):
        return pltpu.make_async_remote_copy(
            src_ref=sout.at[app, q], dst_ref=sin.at[app, q],
            send_sem=ss_sem.at[app, q], recv_sem=sr_sem.at[app, q],
            device_id={"row": nxt}, device_id_type=pl.DeviceIdType.MESH)

    pl.semaphore_wait(barrier, 2)
    for q in range(Q):
        vec_copy(0, q).start()
    pos_copy = pltpu.make_async_remote_copy(
        src_ref=pos, dst_ref=pup, send_sem=ps_sem, recv_sem=pr_sem,
        device_id={"row": prv}, device_id_type=pl.DeviceIdType.MESH)
    pos_copy.start()

    def straddle(ref, q, rows):
        return jnp.concatenate([ref[q, :rows, B:], ref[q + 1, :rows, :B]], axis=1)

    for q in range(Q):
        ze[q] = jnp.zeros(ze.shape[1:], BF16)
        ze[2 * Q + q] = jnp.zeros(ze.shape[1:], BF16)
        if q < Q - 1:
            zo[q] = jnp.zeros(zo.shape[1:], BF16)
            zo[2 * Q + q] = jnp.zeros(zo.shape[1:], BF16)

    def odd_pairs(rows, eo):
        for q in range(Q - 1, 2 * Q):
            odd = straddle(ze, q, rows)
            zo[q, :rows] = odd
            if Q <= q < 2 * Q - 1:
                eo[q - Q] = odd

    odd_pairs(NV, eo0)

    for i in range(C):
        blk[i, K] = jnp.zeros((B, B), BF16)
        blkt[i, K] = jnp.zeros((B, B), BF16)

    @pl.loop(0, C)
    def _(i):
        block_copy(i).wait()
        for k in range(K):
            blkt[i, k] = blk[i, k].T

    table_copy.wait()

    def across(ref, start, rows):
        return [ref[start + m, :rows] for m in range(Q)]

    for app, (ee, eo) in enumerate(((ee0, eo0), (ee1, eo1), (ee2, eo2))):
        M = 2 * NV if app == 2 else NV
        if app == 2:
            pos_copy.wait()

        @pl.loop(0, C // STEP)
        def _(s):
            spills = []
            for h in range(STEP):
                j = STEP * s + h
                t = (STEP // 2) * s + h // 2
                z = (ze, zo)[h % 2]
                lhs = jnp.concatenate(
                    [jnp.concatenate(across(z, t, M), axis=1),
                     jnp.concatenate(across(z, t + Q, M), axis=1)], axis=0)
                rows = [lax.rem(j + C - d, C) for d in range(K, 0, -1)]
                rhs = jnp.concatenate(
                    [blk[i, table[i, K - m]] for m, i in enumerate(rows)], axis=0)
                acc = jnp.dot(lhs, rhs, preferred_element_type=F32)
                own[j, :M] = acc[:M]
                spills.append(acc[M:])
            for g in range(STEP // 2):
                q = (STEP // 2) * s + g
                spill = jnp.concatenate(spills[2 * g:2 * g + 2], axis=1)
                if app == 2:
                    spill = pup[pl.ds(q, 1), :] * spill[:NV] - spill[NV:]
                sout[app, q] = spill.astype(BF16)
                spill_copy(app, q).start()

        @pl.loop(0, C // STEP)
        def _(s):
            for g in range(STEP // 2):
                q = (STEP // 2) * s + g
                vec_copy(app, q).wait_recv()
                if app == 2:
                    up = pup[pl.ds(q, 1), :] * ee[Q + q, :NV].astype(F32)
                    ee[Q + q, NV:] = up.astype(BF16)
                eo[Q - 1 + q] = straddle(ee, Q - 1 + q, M)
            sums = []
            for h in range(STEP):
                j = STEP * s + h
                t = (STEP // 2) * s + h // 2
                last = ee[t + Q]
                last = last[:, B:] if h % 2 else last[:, :B]
                lhs = jnp.concatenate(
                    across((ee, eo)[h % 2], t, M) + [last], axis=1)
                rhs = jnp.concatenate(
                    [blkt[j, table[j, d]] for d in range(K + 1)], axis=0)
                sums.append(own[j, :M] + jnp.dot(
                    lhs, rhs, preferred_element_type=F32))
            for g in range(STEP // 2):
                q = (STEP // 2) * s + g
                total = jnp.concatenate(sums[2 * g:2 * g + 2], axis=1)
                spill_copy(app, q).wait_recv()
                arriving = sin[app, q].astype(F32)
                if app == 0:
                    x1 = (total + arriving).astype(BF16)
                    ee1[q] = x1
                    vec_copy(1, q).start()
                    ze[Q + q, :NV] = x1
                elif app == 1:
                    x2 = 2.0 * (total + arriving) - ee0[q].astype(F32)
                    x2 = x2.astype(BF16)
                    ee2[q, :NV] = x2
                    vec_copy(2, q).start()
                    scaled = (pos[pl.ds(q, 1), :] * x2.astype(F32)).astype(BF16)
                    ee2[q, NV:] = scaled
                    ze[Q + q, :NV] = x2
                    ze[Q + q, NV:] = scaled
                    x2_ref[:, pl.ds(pl.multiple_of(q * W, 128), W)] = x2
                else:
                    weight = pos[pl.ds(q, 1), :]
                    heat = weight * total[:NV] - total[NV:] + arriving
                    heat_ref[:, pl.ds(pl.multiple_of(q * W, 128), W)] = heat

        if app == 0:
            odd_pairs(NV, eo1)
        elif app == 1:
            odd_pairs(2 * NV, eo2)

    for app in range(3):
        for q in range(Q):
            vec_copy(app, q).wait_send()
            spill_copy(app, q).wait_send()


def body(start_vectors, blocks, block_cols, positions):
    C, K, B = blocks.shape[0], blocks.shape[1], blocks.shape[2]
    NV = start_vectors.shape[0]
    Q, W = C // 2, 2 * B
    rows = -(-Q // 8) * 8
    vmem = pl.BlockSpec(memory_space=pltpu.VMEM)
    dma = pltpu.SemaphoreType.DMA
    pairs = lambda count, m: pltpu.VMEM((count, m, W), BF16)
    return tuple(pl.pallas_call(
        kernel,
        out_shape=(jax.ShapeDtypeStruct(start_vectors.shape, BF16),
                   jax.ShapeDtypeStruct(start_vectors.shape, F32)),
        in_specs=[vmem, vmem, vmem, pl.BlockSpec(memory_space=pl.ANY)],
        out_specs=(vmem, vmem),
        scratch_shapes=[
            pltpu.VMEM((C, K + 1, B, B), BF16), pltpu.VMEM((C, K + 1, B, B), BF16),
            pairs(3 * Q, 2 * NV), pairs(3 * Q, 2 * NV),
            pairs(2 * Q, NV), pairs(2 * Q, NV),
            pairs(2 * Q, NV), pairs(2 * Q, NV),
            pairs(2 * Q, 2 * NV), pairs(2 * Q, 2 * NV),
            pltpu.VMEM((C, 2 * NV, B), F32),
            pltpu.VMEM((3, Q, NV, W), BF16), pltpu.VMEM((3, Q, NV, W), BF16),
            pltpu.VMEM((rows, W), F32), pltpu.VMEM((rows, W), F32),
            pltpu.VMEM((C, 128), jnp.int32), pltpu.SMEM((C, 128), jnp.int32),
            dma((C,)), dma((3, Q)), dma((3, Q)), dma((3, Q)), dma((3, Q)),
            dma, dma, dma,
        ],
        compiler_params=pltpu.CompilerParams(
            collective_id=0, has_side_effects=True, vmem_limit_bytes=56 * 1024 * 1024),
    )(block_cols, start_vectors, positions.reshape(1, -1), blocks))


def solution(mesh):
    return jax.shard_map(
        body,
        mesh=mesh,
        in_specs=(
            P(None, ("grp", "row")),
            P(("grp", "row"), None, None, None),
            P(("grp", "row"), None),
            P(("grp", "row")),
        ),
        out_specs=(P(None, ("grp", "row")), P(None, ("grp", "row"))),
        check_vma=False,
    )
```

profile of v0, /device:TPU:0, one launch (start us, length us, event | category | flops | bytes accessed | tf_op | source)
XLA Modules:
  0.0 40.3 jit_solution(17574429174218379372)
XLA Ops:
  0.6 1.3 %reshape.7.p_ref = bf16[1,2304]{1,0:T(2,128)(2,1)} reshape(bf16[2304]{0:T(1024)(128)(2,1)} %param.7) | data formatting | bytes 9216 | tf_op jit(solution)/shard_map/reshape | solution.py:227
  1.9 34.7 %shard_map.59 = (bf16[64,2304]{1,0:T(8,128)(2,1)}, f32[64,2304]{1,0:T(8,128)}) custom-call(s32[12,12]{1,0:T(8,128)} %cols_ref.1, bf16[64,2304]{1,0:T(8,128)(2,1)} %v_ref.1, bf16[1,2304]{1,0:T(2,128)(2,1)} %reshape.7.p_ref, bf16[12,12,192,192]{3,2,1,0:T(8,128)(2,1)} %blocks_ref.1), custom_call_target="tpu_custom_call" | custom-call | tf_op jit(solution)/shard_map/pallas_call | solution.py:206
  36.7 1.7 %copy.8 = bf16[64,2304]{1,0:T(8,128)(2,1)} copy(bf16[64,2304]{1,0:T(8,128)(2,1)} %get-tuple-element.4) | data formatting | bytes 589824
  38.4 1.9 %copy.9 = f32[64,2304]{1,0:T(8,128)} copy(f32[64,2304]{1,0:T(8,128)} %get-tuple-element.5) | data formatting | bytes 1179648
where the time goes:
time: 40.5 us; the launch traced here: 40.3 us
  Pallas kernels  34.7 us (86%)
  local copies, waits for them, and re-layouts  4.91 us (12%)
  between operations  0.64 us (2%)
    pallas_call x1, Pallas kernels, body(): pl.pallas_call(kernel, out_shape=(jax.ShapeDtypeStruct(start_vectors.shap...  34.7 us
    unnamed x2, local copies, waits for them, and re-layouts  3.61 us
    reshape x1, local copies, waits for them, and re-layouts, body(): positions.reshape(1, -1)  1.3 us

commit v1 on v0

--- a/solution.py
+++ b/solution.py
@@ -7,7 +7,9 @@
 
 F32 = jnp.float32
 BF16 = jnp.bfloat16
-STEP = 4
+STEP = 6
+GROUP = 2
+LATE = True
 
 
 def kernel(cols_ref, v_ref, p_ref, blocks_ref, x2_ref, heat_ref,
@@ -51,8 +53,10 @@
         ee0[q] = pair
         ze[Q + q, :NV] = pair
     pos[...] = jnp.zeros(pos.shape, F32)
+    lines = p_ref[...].astype(F32)
     for q in range(Q):
-        pos[q:q + 1, :] = p_ref[:, q * W:(q + 1) * W].astype(F32)
+        pos[q:q + 1, :] = jnp.concatenate(
+            [lines[r:r + 1] for r in range(q * W // 128, (q + 1) * W // 128)], axis=1)
 
     def vec_copy(app, q):
         e = (ee0, ee1, ee2)[app]
@@ -114,43 +118,68 @@
         if app == 2:
             pos_copy.wait()
 
-        @pl.loop(0, C // STEP)
-        def _(s):
-            spills = []
-            for h in range(STEP):
-                j = STEP * s + h
-                t = (STEP // 2) * s + h // 2
-                z = (ze, zo)[h % 2]
-                lhs = jnp.concatenate(
-                    [jnp.concatenate(across(z, t, M), axis=1),
-                     jnp.concatenate(across(z, t + Q, M), axis=1)], axis=0)
-                rows = [lax.rem(j + C - d, C) for d in range(K, 0, -1)]
+        if app < 2:
+            @pl.loop(0, C // STEP)
+            def _(s):
+                spills = []
+                for h in range(STEP):
+                    j = STEP * s + h
+                    t = (STEP // 2) * s + h // 2
+                    z = (ze, zo)[h % 2]
+                    lhs = jnp.concatenate(
+                        [jnp.concatenate(across(z, t, M), axis=1),
+                         jnp.concatenate(across(z, t + Q, M), axis=1)], axis=0)
+                    rows = [lax.rem(j + C - d, C) for d in range(K, 0, -1)]
+                    rhs = jnp.concatenate(
+                        [blk[i, table[i, K - m]] for m, i in enumerate(rows)], axis=0)
+                    acc = jnp.dot(lhs, rhs, preferred_element_type=F32)
+                    own[j, :M] = acc[:M]
+                    spills.append(acc[M:])
+                for g in range(STEP // 2):
+                    q = (STEP // 2) * s + g
+                    spill = jnp.concatenate(spills[2 * g:2 * g + 2], axis=1)
+                    sout[app, q] = spill.astype(BF16)
+                    spill_copy(app, q).start()
+
+        else:
+            def mirrored(j, low, high):
+                count = high - low
+                src = eo if low % 2 else ee
+                parts = [src[low // 2 + m] for m in range(count // 2)]
+                if count % 2:
+                    last = ee[(high - 1) // 2]
+                    parts.append(last[:, :B] if high % 2 else last[:, B:])
+                lhs = jnp.concatenate(parts, axis=1)
                 rhs = jnp.concatenate(
-                    [blk[i, table[i, K - m]] for m, i in enumerate(rows)], axis=0)
-                acc = jnp.dot(lhs, rhs, preferred_element_type=F32)
-                own[j, :M] = acc[:M]
-                spills.append(acc[M:])
-            for g in range(STEP // 2):
-                q = (STEP // 2) * s + g
-                spill = jnp.concatenate(spills[2 * g:2 * g + 2], axis=1)
-                if app == 2:
-                    spill = pup[pl.ds(q, 1), :] * spill[:NV] - spill[NV:]
+                    [blk[i, table[i, (j - i) % C if j != i else C]]
+                     for i in range(low, high)], axis=0)
+                return jnp.dot(lhs, rhs, preferred_element_type=F32)
+
+            for q in range(Q):
+                pair = []
+                for j in (2 * q, 2 * q + 1):
+                    pair.append(mirrored(j, j, C))
+                    if j:
+                        own[j] = mirrored(j, 0, j)
+                    else:
+                        own[j] = jnp.zeros(own.shape[1:], F32)
+                spill = jnp.concatenate(pair, axis=1)
+                spill = pup[q:q + 1, :] * spill[:NV] - spill[NV:]
                 sout[app, q] = spill.astype(BF16)
                 spill_copy(app, q).start()
 
-        @pl.loop(0, C // STEP)
-        def _(s):
-            for g in range(STEP // 2):
-                q = (STEP // 2) * s + g
+        def products(s):
+            for g in range(GROUP // 2):
+                q = (GROUP // 2) * s + g
                 vec_copy(app, q).wait_recv()
                 if app == 2:
-                    up = pup[pl.ds(q, 1), :] * ee[Q + q, :NV].astype(F32)
+                    up = pup[q:q + 1, :] * ee[Q + q, :NV].astype(F32)
                     ee[Q + q, NV:] = up.astype(BF16)
                 eo[Q - 1 + q] = straddle(ee, Q - 1 + q, M)
             sums = []
-            for h in range(STEP):
-                j = STEP * s + h
-                t = (STEP // 2) * s + h // 2
+            for h in range(GROUP):
+                j = GROUP * s + h
+                t = (GROUP // 2) * s + h // 2
                 last = ee[t + Q]
                 last = last[:, B:] if h % 2 else last[:, :B]
                 lhs = jnp.concatenate(
@@ -159,8 +188,11 @@
                     [blkt[j, table[j, d]] for d in range(K + 1)], axis=0)
                 sums.append(own[j, :M] + jnp.dot(
                     lhs, rhs, preferred_element_type=F32))
-            for g in range(STEP // 2):
-                q = (STEP // 2) * s + g
+            return sums
+
+        def finish(s, sums):
+            for g in range(GROUP // 2):
+                q = (GROUP // 2) * s + g
                 total = jnp.concatenate(sums[2 * g:2 * g + 2], axis=1)
                 spill_copy(app, q).wait_recv()
                 arriving = sin[app, q].astype(F32)
@@ -174,25 +206,44 @@
                     x2 = x2.astype(BF16)
                     ee2[q, :NV] = x2
                     vec_copy(2, q).start()
-                    scaled = (pos[pl.ds(q, 1), :] * x2.astype(F32)).astype(BF16)
+                    scaled = (pos[q:q + 1, :] * x2.astype(F32)).astype(BF16)
                     ee2[q, NV:] = scaled
-                    ze[Q + q, :NV] = x2
-                    ze[Q + q, NV:] = scaled
-                    x2_ref[:, pl.ds(pl.multiple_of(q * W, 128), W)] = x2
+                    x2_ref[:, q * W:(q + 1) * W] = x2
                 else:
-                    weight = pos[pl.ds(q, 1), :]
+                    weight = pos[q:q + 1, :]
                     heat = weight * total[:NV] - total[NV:] + arriving
-                    heat_ref[:, pl.ds(pl.multiple_of(q * W, 128), W)] = heat
+                    heat_ref[:, q * W:(q + 1) * W] = heat
+
+        waiting = None
+        for s in range(C // GROUP):
+            sums = products(s)
+            if LATE and waiting is not None:
+                finish(s - 1, waiting)
+            if not LATE:
+                finish(s, sums)
+            waiting = sums
+        if LATE:
+            finish(C // GROUP - 1, waiting)
 
         if app == 0:
             odd_pairs(NV, eo1)
         elif app == 1:
-            odd_pairs(2 * NV, eo2)
+            for q in range(Q - 1):
+                eo2[q] = straddle(ee2, q, 2 * NV)
 
     for app in range(3):
         for q in range(Q):
             vec_copy(app, q).wait_send()
             spill_copy(app, q).wait_send()
+
+
+def hand_over(a_ref, b_ref, a_out, b_out, sem):
+    copies = [pltpu.make_async_copy(a_ref, a_out, sem.at[0]),
+              pltpu.make_async_copy(b_ref, b_out, sem.at[1])]
+    for copy in copies:
+        copy.start()
+    for copy in copies:
+        copy.wait()
 
 
 def body(start_vectors, blocks, block_cols, positions):
@@ -203,7 +254,7 @@
     vmem = pl.BlockSpec(memory_space=pltpu.VMEM)
     dma = pltpu.SemaphoreType.DMA
     pairs = lambda count, m: pltpu.VMEM((count, m, W), BF16)
-    return tuple(pl.pallas_call(
+    results = pl.pallas_call(
         kernel,
         out_shape=(jax.ShapeDtypeStruct(start_vectors.shape, BF16),
                    jax.ShapeDtypeStruct(start_vectors.shape, F32)),
@@ -211,7 +262,7 @@
         out_specs=(vmem, vmem),
         scratch_shapes=[
             pltpu.VMEM((C, K + 1, B, B), BF16), pltpu.VMEM((C, K + 1, B, B), BF16),
-            pairs(3 * Q, 2 * NV), pairs(3 * Q, 2 * NV),
+            pairs(3 * Q, NV), pairs(3 * Q, NV),
             pairs(2 * Q, NV), pairs(2 * Q, NV),
             pairs(2 * Q, NV), pairs(2 * Q, NV),
             pairs(2 * Q, 2 * NV), pairs(2 * Q, 2 * NV),
@@ -224,7 +275,15 @@
         ],
         compiler_params=pltpu.CompilerParams(
             collective_id=0, has_side_effects=True, vmem_limit_bytes=56 * 1024 * 1024),
-    )(block_cols, start_vectors, positions.reshape(1, -1), blocks))
+    )(block_cols, start_vectors, positions.reshape(-1, 128), blocks)
+    anywhere = pl.BlockSpec(memory_space=pl.ANY)
+    return tuple(pl.pallas_call(
+        hand_over,
+        out_shape=tuple(jax.ShapeDtypeStruct(r.shape, r.dtype) for r in results),
+        in_specs=[vmem, vmem],
+        out_specs=(anywhere, anywhere),
+        scratch_shapes=[dma((2,))],
+    )(*results))
 
 
 def solution(mesh):

time: 40.5 us -> 36.5 us (0.901)
  local copies, waits for them, and re-layouts: 4.91 us -> 0 us
  Pallas kernels: 34.7 us -> 35.5 us
    unnamed x2 -> x0, local copies, waits for them, and re-layouts: 3.61 us -> none
    pallas_call x0 -> x1, Pallas kernels: none -> 2.09 us  [body(): pl.pallas_call(hand_over, out_shape=tuple((jax.ShapeDtypeStruct(r.shape,...]
    pallas_call x1, Pallas kernels: 34.7 us -> 33.4 us  [body(): pl.pallas_call(kernel, out_shape=(jax.ShapeDtypeStruct(start_vectors.shap...]
    reshape x1 -> x0, local copies, waits for them, and re-layouts: 1.3 us -> none  [body(): positions.reshape(1, -1)]
where the time goes in v1:
time: 36.5 us; the launch traced here: 36.3 us
  Pallas kernels  35.5 us (97%)
  between operations  0.8 us (2%)
    pallas_call x1, Pallas kernels, body(): pl.pallas_call(kernel, out_shape=(jax.ShapeDtypeStruct(start_vectors.shap...  33.4 us
    pallas_call x1, Pallas kernels, body(): pl.pallas_call(hand_over, out_shape=tuple((jax.ShapeDtypeStruct(r.shape,...  2.09 us

profile of v1, /device:TPU:0, one launch (start us, length us, event | category | flops | bytes accessed | tf_op | source)
XLA Modules:
  0.0 36.3 jit_solution(4531557142268243690)
XLA Ops:
  0.6 33.4 %shard_map.59 = (bf16[64,2304]{1,0:T(8,128)(2,1)}, f32[64,2304]{1,0:T(8,128)}) custom-call(s32[12,12]{1,0:T(8,128)} %cols_ref.1, bf16[64,2304]{1,0:T(8,128)(2,1)} %v_ref.1, bf16[18,128]{1,0:T(8,128)(2,1)} %bitcast.1, bf16[12,12,192,192]{3,2,1,0:T(8,128)(2,1)} %blocks_ref.1), custom_call_target="tpu_custom_call" | custom-call | tf_op jit(solution)/shard_map/pallas_call | solution.py:257
  34.1 2.1 %shard_map.60 = (bf16[64,2304]{1,0:T(8,128)(2,1)}, f32[64,2304]{1,0:T(8,128)}) custom-call(bf16[64,2304]{1,0:T(8,128)(2,1)} %get-tuple-element.4.a_ref, f32[64,2304]{1,0:T(8,128)} %get-tuple-element.5.b_ref), custom_call_target="tpu_custom_call" | custom-call | tf_op jit(solution)/shard_map/pallas_call | solution.py:280

commit v2 on v1

--- a/solution.py
+++ b/solution.py
@@ -135,11 +135,9 @@
                     acc = jnp.dot(lhs, rhs, preferred_element_type=F32)
                     own[j, :M] = acc[:M]
                     spills.append(acc[M:])
-                for g in range(STEP // 2):
-                    q = (STEP // 2) * s + g
-                    spill = jnp.concatenate(spills[2 * g:2 * g + 2], axis=1)
-                    sout[app, q] = spill.astype(BF16)
-                    spill_copy(app, q).start()
+                    if h % 2:
+                        sout[app, t] = jnp.concatenate(spills[-2:], axis=1).astype(BF16)
+                        spill_copy(app, t).start()
 
         else:
             def mirrored(j, low, high):

time: 36.5 us -> 37.9 us (1.038)
  Pallas kernels: 35.5 us -> 36.9 us
    pallas_call x1, Pallas kernels: 33.4 us -> 34.8 us  [body(): pl.pallas_call(kernel, out_shape=(jax.ShapeDtypeStruct(start_vectors.shap...]
where the time goes in v2:
time: 37.9 us; the launch traced here: 37.7 us
  Pallas kernels  36.9 us (97%)
  between operations  0.8 us (2%)
    pallas_call x1, Pallas kernels, body(): pl.pallas_call(kernel, out_shape=(jax.ShapeDtypeStruct(start_vectors.shap...  34.8 us
    pallas_call x1, Pallas kernels, body(): pl.pallas_call(hand_over, out_shape=tuple((jax.ShapeDtypeStruct(r.shape,...  2.09 us

profile of v2, /device:TPU:0, one launch (start us, length us, event | category | flops | bytes accessed | tf_op | source)
XLA Modules:
  0.0 37.7 jit_solution(7082133007777755853)
XLA Ops:
  0.6 34.8 %shard_map.59 = (bf16[64,2304]{1,0:T(8,128)(2,1)}, f32[64,2304]{1,0:T(8,128)}) custom-call(s32[12,12]{1,0:T(8,128)} %cols_ref.1, bf16[64,2304]{1,0:T(8,128)(2,1)} %v_ref.1, bf16[18,128]{1,0:T(8,128)(2,1)} %bitcast.1, bf16[12,12,192,192]{3,2,1,0:T(8,128)(2,1)} %blocks_ref.1), custom_call_target="tpu_custom_call" | custom-call | tf_op jit(solution)/shard_map/pallas_call | solution.py:255
  35.4 2.1 %shard_map.60 = (bf16[64,2304]{1,0:T(8,128)(2,1)}, f32[64,2304]{1,0:T(8,128)}) custom-call(bf16[64,2304]{1,0:T(8,128)(2,1)} %get-tuple-element.4.a_ref, f32[64,2304]{1,0:T(8,128)} %get-tuple-element.5.b_ref), custom_call_target="tpu_custom_call" | custom-call | tf_op jit(solution)/shard_map/pallas_call | solution.py:278
